TPU v7x, 128 devices: a whole 4x4x4 slice. The times are simulated.
128 devices in a mesh: dp: 32 (over x, z, core), owner: 4 (over y).
Axes of the slice: x: 4, y: 4, z: 4, core: 2. Of those that a mesh axis runs over, the one named last changes fastest.
Arguments:
- hidden: bfloat16 [32768, 6912], P(('dp', 'owner')), may hold values from -6 to 6
- grad_out: bfloat16 [32768, 2560], P(('dp', 'owner')), may hold values from -6 to 6
- block_list: int32 [512, 2], replicated, may hold values from 0 to 107, as said below
- live_block_count: int32 [128], replicated, may hold values from 1 to 4, as said below
- master: float32 [512, 4096], P(('dp', 'owner')), may hold values from -6 to 6
- moment: float32 [512, 4096], P(('dp', 'owner')), may hold values from -6 to 6
- variance: float32 [512, 4096], P(('dp', 'owner')), may hold values from 0.25 to 4
Outputs:
- new_master: float32 [512, 4096], P(('dp', 'owner'))
- new_moment: float32 [512, 4096], P(('dp', 'owner'))
- new_variance: float32 [512, 4096], P(('dp', 'owner'))
- clipped_grad: float32 [512, 4096], P(('dp', 'owner'))
- published: bfloat16 [512, 4096], replicated
Inputs may be any that keep to these rules, and one draw needn't show every extreme that they name: `block_list`: each row names a block: its row index below 108, its column index below 40; all rows name different blocks. Rows 4 o to 4 o + 3 are owner o's slots; owner o is the device whose index along dp is o // 4 and whose index along the mesh axis `owner` is o mod 4. Owner o's first live_block_count[o] slots are live, the rest padding; some owner's slots are all live.
All inputs are finite; a program needn't handle non-finite values.
Results may differ from a plain program's by a relative error of at most 0.001.
Values may be sent and summed in bfloat16 or wider, within the bound.
A program may use at most 128 MiB of HBM per device.

v0:
```python
import math

import jax
import jax.numpy as jnp
from jax import lax
from jax.sharding import PartitionSpec as P

BLOCK_SIDE_SIZE = 64
OWNER_SLOTS = 4


def block_terms(hidden, grad_out, row_indices, column_indices, active_slot_mask, row_count):
    tok_rows = hidden.shape[0]
    block_side = BLOCK_SIDE_SIZE
    group_size = math.gcd(row_count, 8 * OWNER_SLOTS)
    hidden_blocks = hidden.reshape(tok_rows, hidden.shape[1] // block_side, block_side)
    output_blocks = grad_out.reshape(tok_rows, grad_out.shape[1] // block_side, block_side)

    def one_group(id_pair):
        row_sel, col_sel = id_pair
        left_cols = jnp.take(hidden_blocks, row_sel, axis=1)
        right_cols = jnp.take(output_blocks, col_sel, axis=1)
        products = lax.dot_general(
            left_cols, right_cols, (((0,), (0,)), ((1,), (1,))), preferred_element_type=jnp.float32
        )
        return products.reshape(group_size, block_side * block_side)

    group_terms = lax.map(
        one_group, (row_indices.reshape(-1, group_size), column_indices.reshape(-1, group_size))
    )
    group_terms = group_terms.reshape(row_count, block_side * block_side)
    return jnp.where(active_slot_mask[:, None], group_terms, jnp.zeros_like(group_terms))


def local(hidden, grad_out, block_list, live_block_count, master, moment, variance):
    slot_rows = master.shape[0]
    row_indices = block_list[:, 0]
    column_indices = block_list[:, 1]
    active_slot_mask = (
        jnp.arange(slot_rows, dtype=jnp.int32)[None, :] < live_block_count[:, None]
    ).reshape(-1)
    weight_gradient = lax.psum_scatter(
        block_terms(
            hidden,
            grad_out,
            row_indices,
            column_indices,
            active_slot_mask,
            lax.axis_size(("dp", "owner")) * slot_rows,
        ),
        ("dp", "owner"),
        scatter_dimension=0,
        tiled=True,
    )
    square_total = lax.psum(jnp.sum(weight_gradient * weight_gradient), ("dp", "owner"))
    live_total = jnp.sum(live_block_count).astype(jnp.float32) * weight_gradient.shape[1]
    mean_square = square_total / live_total
    clip_scale = jnp.minimum(1.0, 1.0 / jnp.sqrt(mean_square + 1e-06))
    clipped_grad = clip_scale * weight_gradient
    new_moment = 0.9 * moment + 0.1 * clipped_grad
    new_variance = 0.95 * variance + 0.05 * clipped_grad * clipped_grad
    moment_hat = new_moment / (1.0 - 0.9**20)
    variance_hat = new_variance / (1.0 - 0.95**20)
    new_master = master - 0.02 * (moment_hat / (jnp.sqrt(variance_hat) + 1e-08) + 0.1 * master)
    own_blocks = new_master.astype(jnp.bfloat16)
    published = lax.all_gather(own_blocks, ("dp", "owner"), axis=0, tiled=True)
    return (new_master, new_moment, new_variance, clipped_grad, published)


def solution(mesh):
    return jax.shard_map(
        local,
        mesh=mesh,
        in_specs=(
            P(("dp", "owner"), None),
            P(("dp", "owner"), None),
            P(),
            P(),
            P(("dp", "owner"), None),
            P(("dp", "owner"), None),
            P(("dp", "owner"), None),
        ),
        out_specs=(
            P(("dp", "owner"), None),
            P(("dp", "owner"), None),
            P(("dp", "owner"), None),
            P(("dp", "owner"), None),
            P(),
        ),
        check_vma=False,
    )
```

profile of v0, /device:TPU:1, one launch (start us, length us, event | category | flops | bytes accessed | tf_op | source)
XLA Modules:
  0.0 451.4 jit_solution(7616821432423559366)
XLA Ops:
  8.2 6.0 %copy.16 = bf16[256,6912]{0,1:T(8,128)(2,1)} copy(bf16[256,6912]{1,0:T(8,128)(2,1)} %param.9) | data formatting | bytes 7077888 | tf_op args[0]
  14.1 1.6 copy.17
  15.7 115.8 %while.10 = (s32[]{:T(128)}, f32[16,32,4096]{2,1,0:T(8,128)}, s32[16,32]{1,0:T(8,128)S(1)}, bf16[256,108,64]{0,2,1:T(8,128)(2,1)}, s32[16,32]{1,0:T(8,128)S(1)}, /*index=5*/bf16[256,40,64]{0,2,1:T(8,128)(2,1)S(1)}, s32[]{:T(128)}) while((s32[]{:T(128)}, f32[16,32,4096]{2,1,0:T(8,128)}, s32[16,32]{1,0:T(8,128)S(1)}, ...), condition=%wide.region_1.2_spmd, body=%wide.region_0.1_spmd.sunk | while | flops 68160064 | bytes 8923093 | solution.py:28
  16.4 2.6 gather_fusion.1
  19.1 1.5 fusion.20
  20.6 1.6 broadcast_in_dim.44
  22.2 0.9 constant_dynamic-update-slice_fusion.2
  23.7 2.6 gather_fusion.1
  26.3 1.5 fusion.20
  27.8 1.6 broadcast_in_dim.44
  29.4 0.9 constant_dynamic-update-slice_fusion.2
  31.0 2.6 gather_fusion.1
  33.6 1.5 fusion.20
  35.1 1.6 broadcast_in_dim.44
  38.2 2.6 gather_fusion.1
  40.9 1.5 fusion.20
  42.4 1.6 broadcast_in_dim.44
  45.4 2.6 gather_fusion.1
  48.1 1.5 fusion.20
  49.6 1.6 broadcast_in_dim.44
  51.2 0.9 constant_dynamic-update-slice_fusion.2
  52.7 2.6 gather_fusion.1
  55.3 1.5 fusion.20
  56.8 1.6 broadcast_in_dim.44
  59.9 2.6 gather_fusion.1
  62.6 1.5 fusion.20
  64.1 1.6 broadcast_in_dim.44
  67.1 2.6 gather_fusion.1
  69.8 1.5 fusion.20
  71.3 1.6 broadcast_in_dim.44
  74.4 2.6 gather_fusion.1
  77.0 1.5 fusion.20
  78.5 1.6 broadcast_in_dim.44
  80.1 0.9 constant_dynamic-update-slice_fusion.2
  81.6 2.6 gather_fusion.1
  84.3 1.5 fusion.20
  85.8 1.6 broadcast_in_dim.44
  87.3 0.9 constant_dynamic-update-slice_fusion.2
  88.9 2.6 gather_fusion.1
  91.5 1.5 fusion.20
  93.0 1.6 broadcast_in_dim.44
  96.1 2.6 gather_fusion.1
  98.7 1.5 fusion.20
  100.2 1.6 broadcast_in_dim.44
  103.3 2.6 gather_fusion.1
  106.0 1.5 fusion.20
  107.5 1.6 broadcast_in_dim.44
  109.0 0.9 constant_dynamic-update-slice_fusion.2
  110.5 2.6 gather_fusion.1
  113.2 1.5 fusion.20
  114.7 1.6 broadcast_in_dim.44
  117.8 2.6 gather_fusion.1
  120.4 1.5 fusion.20
  121.9 1.6 broadcast_in_dim.44
  125.0 2.6 gather_fusion.1
  127.7 1.5 fusion.20
  129.1 1.6 broadcast_in_dim.44
  131.8 8.2 %bitcast_select_fusion = f32[512,4096]{1,0:T(8,128)} fusion(f32[16,32,4096]{2,1,0:T(8,128)} %get-tuple-element.37, pred[512]{0:T(512)(128)(4,1)S(1)} %lt.64), kind=kLoop, calls=%fused_computation.24 | loop fusion | flops 2097152 | bytes 16777728 | tf_op jit(solution)/shard_map/jit(_where)/select_n | solution.py:32
  141.4 163.7 %all-reduce.3.cloned.1.call-done = f32[512,4096]{1,0:T(8,128)} async-done(((f32[512,4096]{1,0:T(8,128)}), f32[512,4096]{1,0:T(8,128)}) %all-reduce.3.cloned.1.call-update) | async-done | bytes 8388624
  305.1 1.5 multiply_reduce_fusion
  306.7 64.0 %psum.7 = f32[]{:T(128)} all-reduce(f32[]{:T(128)} %multiply_reduce_fusion), channel_id=1, replica_groups=mesh['dp'=32,'owner'=4] {'dp','owner'}, use_global_device_ids=true, to_apply=%region_4.5 | all-reduce | flops 1 | bytes 8 | tf_op jit(solution)/shard_map/psum | solution.py:55
  371.4 1.7 convert_bitcast_fusion
  373.1 64.5 %all-gather.3.cloned.1.call-done = bf16[128,4,4096]{2,1,0:T(4,128)(2,1)} async-done(((bf16[1,4,4096]{2,1,0:T(4,128)(2,1)}), bf16[128,4,4096]{2,1,0:T(4,128)(2,1)}) %all-gather.3.cloned.1.call-update) | async-done | bytes 4194320 | tf_op jit(solution)/shard_map/all_gather | solution.py:66
  437.7 6.9 %reshape.124 = bf16[512,4096]{1,0:T(8,128)(2,1)} reshape(bf16[128,4,4096]{2,1,0:T(4,128)(2,1)} %all-gather.3.cloned.1.call-done) | data formatting | bytes 8388608
  (109 shorter events, 20.7 us)
Async XLA Ops:
  7.2 298.0 %all-reduce.3.cloned.1.call-start = ((), (), s32[]{:S(2)}) async-start(), calls=%async_computation.1 | async-start | bytes 16777216
  15.7 115.8 %copy-start.3 = (s32[128]{0:T(128)S(1)}, s32[128]{0:T(128)}, u32[]{:S(2)}) copy-start(s32[128]{0:T(128)} %param.12) | copy-start | bytes 1540
  140.0 231.4 %copy-start = (f32[4,4096]{1,0:T(4,128)S(1)}, f32[4,4096]{1,0:T(4,128)}, u32[]{:S(2)}) copy-start(f32[4,4096]{1,0:T(4,128)} %param.13) | copy-start | bytes 196612
  140.0 231.4 %copy-start.1 = (f32[4,4096]{1,0:T(4,128)S(1)}, f32[4,4096]{1,0:T(4,128)}, u32[]{:S(2)}) copy-start(f32[4,4096]{1,0:T(4,128)} %param.14) | copy-start | bytes 196612
  140.0 231.4 %copy-start.2 = (f32[4,4096]{1,0:T(4,128)S(1)}, f32[4,4096]{1,0:T(4,128)}, u32[]{:S(2)}) copy-start(f32[4,4096]{1,0:T(4,128)} %param.15) | copy-start | bytes 196612
  140.0 297.6 %all-gather.3.cloned.1.call-start = ((), (), s32[]{:S(2)}) async-start(), calls=%async_computation | async-start | bytes 4227072 | tf_op jit(solution)/shard_map/all_gather | solution.py:66
Sparse Core Ops, SparseCore 0:
  140.2 164.9 all-reduce.2
  373.3 64.3 all-gather.2
where the time goes:
time: 453 us; the launch traced here: 451 us
  waiting for transfers between devices  228 us (50%)
  local copies, waits for them, and re-layouts  106 us (23%)
  blocking collectives  64 us (14%)
  matrix products  24 us (5%)
  between operations  15.5 us (3%)
  other arithmetic  12.8 us (3%)
    unnamed x3, waiting for transfers between devices  164 us
    all_gather x1, waiting for transfers between devices, local(): published = lax.all_gather(own_blocks, ('dp', 'owner'), axis=0, tiled=True)  64.5 us
    psum x1, blocking collectives, local(): lax.psum(jnp.sum(weight_gradient * weight_gradient), ('dp', 'owner'))  64 us
    gather x16, local copies, waits for them, and re-layouts, one_group(): left_cols = jnp.take(hidden_blocks, row_sel, axis=1)  41.9 us
    broadcast_in_dim x16, local copies, waits for them, and re-layouts, block_terms(): lax.map(one_group, (row_indices.reshape(-1, group_size), column_indices.r...  25.3 us
    dot_general x16, matrix products, one_group(): lax.dot_general(left_cols, right_cols, (((0,), (0,)), ((1,), (1,))), pref...  24 us
    unnamed x11, local copies, waits for them, and re-layouts  14.5 us
    dynamic_update_slice x16, local copies, waits for them, and re-layouts, block_terms(): lax.map(one_group, (row_indices.reshape(-1, group_size), column_indices.r...  13.6 us
  transfers between devices with their start and end apart: 2, of which 2 were waited for; matrix products, arithmetic and copies ran while one was open for 0% of the time, Pallas kernels for 0%

commit v1 on v0

v1 whole, which is shorter than its diff:
```python
import functools

import jax
import jax.numpy as jnp
from jax import lax
from jax.experimental import pallas as pl
from jax.experimental.pallas import tpu as pltpu
from jax.sharding import PartitionSpec as P

MESH = pl.DeviceIdType.MESH
SIDE = 64
TOKENS = 256
SLAB_ORDER = (2, 1, 3, 0)
STREAMS = ((0, 48, "xyz"), (48, 48, "yzx"), (96, 32, "zxy"))
F32 = jnp.float32


def where_am_i():
    dp = lax.axis_index("dp")
    y = lax.axis_index("owner")
    return {"x": dp // 8, "z": (dp // 2) % 4, "c": dp % 2, "y": y}


def device_at(place):
    return ((place["x"] * 4 + place["z"]) * 2 + place["c"], place["y"])


def moved(me, **by):
    place = dict(me)
    for axis, step in by.items():
        place[axis] = (me[axis] + step) % (2 if axis == "c" else 4)
    return place


def exponent_of(top):
    top = jnp.maximum(jnp.full((16, 128), jnp.max(top), F32), 1e-30)
    return jnp.ceil(jnp.log2(top * (1.0 / 32000.0)))


def encode(values, inverse):
    return jnp.round(values * inverse).astype(jnp.int32).astype(jnp.int16)


def splat(tile):
    return tile[0:1, :].astype(F32)


def region(buf, stream, level, me, fixed):
    first, rows, _ = stream
    index = [fixed.get(a, slice(None)) for a in "xzcy"]
    return buf.at[(*index, pl.ds(first, rows), slice(None))]


def kernel(
    list_ref, hidden_hbm, grad_out_hbm, live_ref, master_ref, moment_ref, variance_ref,
    new_master_ref, new_moment_ref, new_variance_ref, clipped_ref, published,
    hidden, grad_out, grad_out_t, acc, pair_part, sib_send, sib_recv,
    send1a, recv1a, send1b, recv1b, send1c, recv1c,
    send2a, recv2a, send2b, recv2b, send2c, recv2c,
    send3a, recv3a, send3b, recv3b, send3c, recv3c,
    turned, flat, sum_send, sum_recv,
    load_sem, send_sem, recv_sem,
):
    me = where_am_i()
    px, py, pz, pc = me["x"], me["y"], me["z"], me["c"]
    loads = [
        pltpu.make_async_copy(grad_out_hbm, grad_out, load_sem.at[0]),
        pltpu.make_async_copy(hidden_hbm, hidden, load_sem.at[1]),
    ]
    for load in loads:
        load.start()

    peers = [moved(me, c=1)]
    peers += [moved(me, **{a: d}) for a in "xyz" for d in (1, 2, 3)]
    peers += [moved(me, x=d, c=1) for d in (1, 2, 3)]
    peers += [moved(me, y=i, z=j) for i in (1, 2, 3) for j in (1, 2, 3)]
    barrier = pltpu.get_barrier_semaphore()
    for peer in peers:
        pl.semaphore_signal(barrier, inc=1, device_id=device_at(peer), device_id_type=MESH)

    loads[0].wait()
    for t in range(20):
        grad_out_t[pl.ds(t * 128, 128), :] = grad_out[:, t * 128 : (t + 1) * 128].T
    loads[1].wait()
    pl.semaphore_wait(barrier, len(peers))

    issued = []

    def send(src, dst, to):
        n = len(issued)
        copy = pltpu.make_async_remote_copy(
            src_ref=src, dst_ref=dst, send_sem=send_sem.at[n], recv_sem=recv_sem.at[n],
            device_id=device_at(to), device_id_type=MESH,
        )
        copy.start()
        issued.append(copy)
        return copy

    lane = lax.broadcasted_iota(jnp.int32, (SIDE, 128), 1)

    low = lane < SIDE

    def two_blocks(pair):
        both, odd = [], []
        for slot in (2 * pair, 2 * pair + 1):
            row, column = list_ref[2 * slot], list_ref[2 * slot + 1]
            left = grad_out_t[pl.ds(column * SIDE, SIDE), :]
            right = hidden[:, pl.ds((row >> 1) * 128, 128)]
            both.append(jnp.dot(left, right, preferred_element_type=F32))
            odd.append(row & 1)
        crossed = pltpu.roll(jnp.where(low, both[1], both[0]), SIDE, 1)
        straight = jnp.where(low, both[0], both[1])
        return jnp.where(jnp.where(low, odd[0], 1 - odd[1]) == 1, crossed, straight)

    sends1 = []
    for k, step in enumerate(SLAB_ORDER):
        zk = (pz + step) % 4

        def for_sibling(i, top, zk=zk):
            for u in range(16):
                x, y, p = 2 * i + u // 8, (u // 2) % 4, u % 2
                owner = ((x * 4 + zk) * 2 + (1 - pc)) * 4 + y
                part = two_blocks(2 * owner + p)
                pair_part[x, y, pl.ds(p * SIDE, SIDE), :] = part
                top = jnp.maximum(top, jnp.max(jnp.abs(part).reshape(8, 8, 128), axis=0))
            return top

        top = lax.fori_loop(0, 2, for_sibling, jnp.zeros((8, 128), F32))
        exponent = exponent_of(top)
        inverse = jnp.exp2(-exponent)[0:1, :]
        for x in range(4):
            for y in range(4):
                sib_send[k, pl.ds((x * 4 + y) * 128, 128), :] = encode(pair_part[x, y], inverse)
        sib_send[k, pl.ds(2048, 16), :] = exponent.astype(jnp.int32).astype(jnp.int16)
        sib = send(sib_send.at[k], sib_recv.at[k], moved(me, c=1))

        def for_self(i, carry, zk=zk):
            for u in range(16):
                x, y, p = 2 * i + u // 8, (u // 2) % 4, u % 2
                owner = ((x * 4 + zk) * 2 + pc) * 4 + y
                acc[x, zk, y, pl.ds(p * SIDE, SIDE), :] = two_blocks(2 * owner + p)
            return carry

        lax.fori_loop(0, 2, for_self, 0)
        sib.wait_recv()
        scale = jnp.exp2(splat(sib_recv[k, pl.ds(2048, 16), :]))
        top = jnp.zeros((8, 128), F32)
        for x in range(4):
            for y in range(4):
                total = acc[x, zk, y] + scale * sib_recv[k, pl.ds((x * 4 + y) * 128, 128), :].astype(F32)
                acc[x, zk, y] = total
                top = jnp.maximum(top, jnp.max(jnp.abs(total).reshape(16, 8, 128), axis=0))
        exponent = exponent_of(top)
        inverse = jnp.exp2(-exponent)[0:1, :]
        exponent = exponent.astype(jnp.int32).astype(jnp.int16)
        slab = []
        if step:
            for x in range(4):
                for y in range(4):
                    send1c[step - 1, pl.ds((x * 4 + y) * 32, 32), :] = encode(acc[x, zk, y, 96:128, :], inverse)
            send1c[step - 1, pl.ds(512, 16), :] = exponent
            slab.append(send(send1c.at[step - 1], recv1c.at[step - 1], moved(me, z=step)))
        for d in (2, 1, 3):
            to = (px + d) % 4
            for y in range(4):
                send1a[k, d - 1, pl.ds(y * 48, 48), :] = encode(acc[to, zk, y, 0:48, :], inverse)
            send1a[k, d - 1, pl.ds(192, 16), :] = exponent
            slab.append(send(send1a.at[k, d - 1], recv1a.at[k, d - 1], moved(me, x=d)))
            to = (py + d) % 4
            for x in range(4):
                send1b[k, d - 1, pl.ds(x * 48, 48), :] = encode(acc[x, zk, to, 48:96, :], inverse)
            send1b[k, d - 1, pl.ds(192, 16), :] = exponent
            slab.append(send(send1b.at[k, d - 1], recv1b.at[k, d - 1], moved(me, y=d)))
        sends1.append(slab)

    def finish(k):
        step = SLAB_ORDER[k]
        zk = (pz + step) % 4
        slab = list(sends1[k])
        if step:
            slab.pop(0).wait_recv()
            scale = jnp.exp2(splat(recv1c[step - 1, pl.ds(512, 16), :]))
            for x in range(4):
                for y in range(4):
                    acc[x, pz, y, 96:128, :] += scale * recv1c[step - 1, pl.ds((x * 4 + y) * 32, 32), :].astype(F32)
        for n, d in enumerate((2, 1, 3)):
            slab[2 * n].wait_recv()
            scale = jnp.exp2(splat(recv1a[k, d - 1, pl.ds(192, 16), :]))
            for y in range(4):
                acc[px, zk, y, 0:48, :] += scale * recv1a[k, d - 1, pl.ds(y * 48, 48), :].astype(F32)
            slab[2 * n + 1].wait_recv()
            scale = jnp.exp2(splat(recv1b[k, d - 1, pl.ds(192, 16), :]))
            for x in range(4):
                acc[x, zk, py, 48:96, :] += scale * recv1b[k, d - 1, pl.ds(x * 48, 48), :].astype(F32)

    for k in range(4):
        finish(k)

    def later_phase(axis, out_buf, in_buf, rows, first, count, place):
        held = [[acc[(*place(j, (me[axis] + d) % 4), pl.ds(first, rows), slice(None))] for j in range(count)] for d in (2, 1, 3)]
        top = functools.reduce(jnp.maximum, [jnp.max(jnp.abs(v).reshape(rows // 8, 8, 128), axis=0) for h in held for v in h])
        exponent = exponent_of(top)
        inverse = jnp.exp2(-exponent)[0:1, :]
        exponent = exponent.astype(jnp.int32).astype(jnp.int16)
        copies = []
        for h, d in zip(held, (2, 1, 3), strict=True):
            for j, v in enumerate(h):
                out_buf[d - 1, pl.ds(j * rows, rows), :] = encode(v, inverse)
            out_buf[d - 1, pl.ds(count * rows, 16), :] = exponent
            copies.append(send(out_buf.at[d - 1], in_buf.at[d - 1], moved(me, **{axis: d})))

        def add():
            for d, copy in zip((2, 1, 3), copies, strict=True):
                copy.wait_recv()
                scale = jnp.exp2(splat(in_buf[d - 1, pl.ds(count * rows, 16), :]))
                for j in range(count):
                    acc[(*place(j, me[axis]), pl.ds(first, rows), slice(None))] += scale * in_buf[d - 1, pl.ds(j * rows, rows), :].astype(F32)

        return add

    adds = [
        later_phase("x", send2c, recv2c, 32, 96, 4, lambda j, q: (q, pz, j)),
        later_phase("y", send2a, recv2a, 48, 0, 4, lambda j, q: (px, j, q)),
        later_phase("z", send2b, recv2b, 48, 48, 4, lambda j, q: (j, q, py)),
    ]
    adds[0]()
    last = [later_phase("y", send3c, recv3c, 32, 96, 1, lambda j, q: (px, pz, q))]
    adds[1]()
    last.append(later_phase("z", send3a, recv3a, 48, 0, 1, lambda j, q: (px, q, py)))
    adds[2]()
    last.append(later_phase("x", send3b, recv3b, 48, 48, 1, lambda j, q: (q, pz, py)))
    for add in last:
        add()

    counts = live_ref[0:1, :]
    owner = ((px * 4 + pz) * 2 + pc) * 4 + py
    at = lax.broadcasted_iota(jnp.int32, (1, 128), 1)
    mine = jnp.sum(jnp.where(at == owner, counts, 0.0))
    live_total = jnp.sum(counts) * float(SIDE * SIDE)
    slot = 2 * (lax.broadcasted_iota(jnp.int32, (128, 128), 0) // SIDE) + lax.broadcasted_iota(jnp.int32, (128, 128), 1) // SIDE
    own = jnp.where(slot.astype(F32) < mine, acc[px, pz, py], 0.0)
    sum_send[0] = jnp.full((8, 128), jnp.sum(own * own), F32)
    copies = []
    for n, by in enumerate([{"c": 1}] + [{"x": d, "c": c} for d in (1, 2, 3) for c in (0, 1)]):
        copies.append(send(sum_send.at[0], sum_recv.at[n], moved(me, **by)))
    turned[...] = own.T
    even, odd = turned[pl.ds(0, SIDE, 2), :], turned[pl.ds(1, SIDE, 2), :]
    flat[pl.ds(0, SIDE), :] = jnp.where(lane < SIDE, even, pltpu.roll(odd, SIDE, 1))
    flat[pl.ds(SIDE, SIDE), :] = jnp.where(lane < SIDE, pltpu.roll(even, SIDE, 1), odd)
    square = sum_send[0]
    for n, copy in enumerate(copies):
        copy.wait_recv()
        square += sum_recv[n]
    sum_send[1] = square
    copies = []
    for i in range(4):
        for j in range(4):
            if i or j:
                copies.append(send(sum_send.at[1], sum_recv.at[7 + len(copies)], moved(me, y=i, z=j)))
    for n, copy in enumerate(copies):
        copy.wait_recv()
        square += sum_recv[7 + n]
    mean_square = square[0:4] / live_total
    clip = jnp.minimum(1.0, 1.0 / jnp.sqrt(mean_square + 1e-06))

    for t in range(32):
        at = pl.ds(t * 128, 128)
        clipped = clip * flat[pl.ds(t, 4, 32), :]
        new_moment = 0.9 * moment_ref[:, at] + 0.1 * clipped
        new_variance = 0.95 * variance_ref[:, at] + 0.05 * clipped * clipped
        moment_hat = new_moment / (1.0 - 0.9**20)
        variance_hat = new_variance / (1.0 - 0.95**20)
        master = master_ref[:, at]
        new_master = master - 0.02 * (moment_hat / (jnp.sqrt(variance_hat) + 1e-08) + 0.1 * master)
        clipped_ref[:, at] = clipped
        new_moment_ref[:, at] = new_moment
        new_variance_ref[:, at] = new_variance
        new_master_ref[:, at] = new_master
        turned[pl.ds(t, 4, 32), :] = new_master
    published[px, pz, pc, py] = turned[...].astype(jnp.bfloat16)

    def spread(stream, axis, fixed, d):
        part = region(published, stream, 0, me, fixed)
        return send(part, part, moved(me, **{axis: d}))

    ready = []
    for stream in (STREAMS[0], STREAMS[1], STREAMS[2]):
        axis = stream[2][2]
        ready.append([spread(stream, axis, {"x": px, "y": py, "z": pz, "c": pc}, d) for d in (2, 1, 3)])
    for level in (1, 0):
        for n, stream in enumerate(STREAMS):
            for copy in ready[n]:
                copy.wait_recv()
            fixed = {"c": pc} | {a: me[a] for a in stream[2][: level + 1]}
            axis = stream[2][level]
            ready[n] = [spread(stream, axis, fixed, d) for d in (2, 1, 3)]
    other = moved(me, c=1)
    passed = []
    for stream in STREAMS:
        part = region(published, stream, 0, me, {"c": pc, stream[2][0]: me[stream[2][0]]})
        passed.append(send(part, part, other))
    for m, d in enumerate((1, 3, 2)):
        for n, stream in enumerate(STREAMS):
            ready[n][(2, 1, 3).index(d)].wait_recv()
            part = region(published, stream, 0, me, {"c": pc, stream[2][0]: (me[stream[2][0]] - d) % 4})
            passed.append(send(part, part, other))
    for copy in passed:
        copy.wait_recv()
    for copy in issued:
        copy.wait_send()


def local(hidden, grad_out, block_list, live_block_count, master, moment, variance):
    i16 = jnp.int16
    state = jax.ShapeDtypeStruct(master.shape, F32)
    vmem, hbm = pl.BlockSpec(memory_space=pltpu.VMEM), pl.BlockSpec(memory_space=pl.ANY)
    first = [pltpu.VMEM((4, 3, 208, 128), i16)] * 4 + [pltpu.VMEM((3, 528, 128), i16)] * 2
    second = [pltpu.VMEM((3, 208, 128), i16)] * 4 + [pltpu.VMEM((3, 144, 128), i16)] * 2
    third = [pltpu.VMEM((3, 64, 128), i16)] * 4 + [pltpu.VMEM((3, 48, 128), i16)] * 2
    copies = 4 + 27 + 18 + 22 + 27 + 12
    *updated, published = pl.pallas_call(
        kernel,
        out_shape=[state] * 4 + [jax.ShapeDtypeStruct((4, 4, 2, 4, 128, 128), jnp.bfloat16)],
        in_specs=[pl.BlockSpec(memory_space=pltpu.SMEM), hbm, hbm, vmem, vmem, vmem, vmem],
        out_specs=[vmem] * 5,
        scratch_shapes=[
            pltpu.VMEM(hidden.shape, jnp.bfloat16),
            pltpu.VMEM(grad_out.shape, jnp.bfloat16),
            pltpu.VMEM(grad_out.shape[::-1], jnp.bfloat16),
            pltpu.VMEM((4, 4, 4, 128, 128), F32),
            pltpu.VMEM((4, 4, 128, 128), F32),
            pltpu.VMEM((4, 2064, 128), i16),
            pltpu.VMEM((4, 2064, 128), i16),
            *first, *second, *third,
            pltpu.VMEM((128, 128), F32),
            pltpu.VMEM((128, 128), F32),
            pltpu.VMEM((2, 8, 128), F32),
            pltpu.VMEM((22, 8, 128), F32),
            pltpu.SemaphoreType.DMA((2,)),
            pltpu.SemaphoreType.DMA((copies,)),
            pltpu.SemaphoreType.DMA((copies,)),
        ],
        compiler_params=pltpu.CompilerParams(
            collective_id=0, has_side_effects=True, vmem_limit_bytes=48 * 2**20
        ),
    )(
        block_list.reshape(-1), hidden, grad_out,
        live_block_count.astype(F32).reshape(1, -1), master, moment, variance,
    )
    return (*updated, published.reshape(master.shape[0] * 128, master.shape[1]))


def solution(mesh):
    one, all_of_it = P(("dp", "owner"), None), P()
    return jax.shard_map(
        local,
        mesh=mesh,
        in_specs=(one, one, all_of_it, all_of_it, one, one, one),
        out_specs=(one, one, one, one, all_of_it),
        check_vma=False,
    )
```

time: 453 us -> 87.4 us (0.19)
  waiting for transfers between devices: 228 us -> 0 us
  local copies, waits for them, and re-layouts: 106 us -> 16.6 us
  Pallas kernels: 0 us -> 69 us
  blocking collectives: 64 us -> 0 us
  matrix products: 24 us -> 0 us
  between operations: 15.5 us -> 0.66 us
  other arithmetic: 12.8 us -> 0.66 us
    unnamed x3 -> x0, waiting for transfers between devices: 164 us -> none
    pallas_call x0 -> x1, Pallas kernels: none -> 69 us  [local(): pl.pallas_call(kernel, out_shape=[state] * 4 + [jax.ShapeDtypeStruct((4,...]
    all_gather x1 -> x0, waiting for transfers between devices: 64.5 us -> none  [local(): published = lax.all_gather(own_blocks, ('dp', 'owner'), axis=0, tiled=True)]
    psum x1 -> x0, blocking collectives: 64 us -> none  [local(): lax.psum(jnp.sum(weight_gradient * weight_gradient), ('dp', 'owner'))]
    gather x32 -> x0, local copies, waits for them, and re-layouts: 51.7 us -> none  [the longest x16 41.9 us: one_group(): left_cols = jnp.take(hidden_blocks, row_sel, axis=1)]
    broadcast_in_dim x16 -> x0, local copies, waits for them, and re-layouts: 25.3 us -> none  [block_terms(): lax.map(one_group, (row_indices.reshape(-1, group_size), column_indices.r...]
    dot_general x16 -> x0, matrix products: 24 us -> none  [one_group(): lax.dot_general(left_cols, right_cols, (((0,), (0,)), ((1,), (1,))), pref...]
    dynamic_update_slice x16 -> x0, local copies, waits for them, and re-layouts: 13.6 us -> none  [block_terms(): lax.map(one_group, (row_indices.reshape(-1, group_size), column_indices.r...]
  transfers between devices with their start and end apart: 2 -> 0, of which waited for: 2 -> 0; matrix products, arithmetic and copies ran while one was open for 0% -> 0% of each run, Pallas kernels for 0% -> 0%
where the time goes in v1:
time: 87.4 us; the launch traced here: 86.9 us
  Pallas kernels  69 us (79%)
  local copies, waits for them, and re-layouts  16.6 us (19%)
    pallas_call x1, Pallas kernels, local(): pl.pallas_call(kernel, out_shape=[state] * 4 + [jax.ShapeDtypeStruct((4,...  69 us
    unnamed x15, local copies, waits for them, and re-layouts  9.17 us
    reshape x1, local copies, waits for them, and re-layouts, local(): return (*updated, published.reshape(master.shape[0] * 128, master.shape[1]))  7.28 us

profile of v1, /device:TPU:1, one launch (start us, length us, event | category | flops | bytes accessed | tf_op | source)
XLA Modules:
  0.0 86.9 jit_solution(3859368055572064109)
XLA Ops:
  0.6 0.7 convert_bitcast_fusion.live_ref
  1.3 0.8 copy.12
  2.1 0.2 reshape.19.list_ref
  2.3 0.0 copy-start
  2.3 2.0 %copy-done = bf16[256,6912]{1,0:T(8,128)(2,1)S(1)} copy-done((bf16[256,6912]{1,0:T(8,128)(2,1)S(1)}, bf16[256,6912]{1,0:T(8,128)(2,1)}, u32[]{:S(2)}) %copy-start) | copy-done | bytes 3538968
  4.3 0.0 copy-start.1
  4.3 1.3 %copy-done.1 = bf16[256,2560]{1,0:T(8,128)(2,1)S(1)} copy-done((bf16[256,2560]{1,0:T(8,128)(2,1)S(1)}, bf16[256,2560]{1,0:T(8,128)(2,1)}, u32[]{:S(2)}) %copy-start.1) | copy-done | bytes 1310744
  5.6 0.0 copy-start.2
  5.6 0.8 copy-done.2
  6.5 0.0 copy-start.3
  6.5 0.8 copy-done.3
  7.3 0.0 copy-start.4
  7.3 0.8 copy-done.4
  8.1 69.0 %shard_map.110 = (f32[4,4096]{1,0:T(4,128)S(1)}, f32[4,4096]{1,0:T(4,128)S(1)}, f32[4,4096]{1,0:T(4,128)S(1)}, f32[4,4096]{1,0:T(4,128)S(1)}, bf16[4,4,2,4,128,128]{5,4,3,2,1,0:T(8,128)(2,1)}) custom-call(s32[1024]{0:T(1024)S(1)} %reshape.19.list_ref, bf16[256,6912]{1,0:T(8,128)(2,1)S(1)} %copy-done, bf16[256,2560]{1,0:T(8,128)(2,1)S(1)} %copy-done.1, ...), custom_call_target="tpu_custom_call" | custom-call | tf_op jit(solution)/shard_map/pallas_call | solution.py:321
  77.1 7.3 %reshape.21 = bf16[512,4096]{1,0:T(8,128)(2,1)} reshape(bf16[4,4,2,4,128,128]{5,4,3,2,1,0:T(8,128)(2,1)} %get-tuple-element.14) | data formatting | bytes 8388608 | tf_op jit(solution)/shard_map/reshape | solution.py:350
  84.4 0.6 copy.17
  85.1 0.6 copy.18
  85.7 0.6 copy.19
  86.3 0.6 copy.20
Async XLA Ops:
  2.3 2.0 %copy-start = (bf16[256,6912]{1,0:T(8,128)(2,1)S(1)}, bf16[256,6912]{1,0:T(8,128)(2,1)}, u32[]{:S(2)}) copy-start(bf16[256,6912]{1,0:T(8,128)(2,1)} %hidden_hbm.1) | copy-start | bytes 10616836
  4.3 1.3 %copy-start.1 = (bf16[256,2560]{1,0:T(8,128)(2,1)S(1)}, bf16[256,2560]{1,0:T(8,128)(2,1)}, u32[]{:S(2)}) copy-start(bf16[256,2560]{1,0:T(8,128)(2,1)} %grad_out_hbm.1) | copy-start | bytes 3932164
  5.6 0.8 copy-start.2
  6.5 0.8 copy-start.3
  7.3 0.8 copy-start.4

commit v2 on v1

--- a/solution.py
+++ b/solution.py
@@ -45,27 +45,37 @@
     return tile[0:1, :].astype(F32)
 
 
-def region(buf, stream, level, me, fixed):
-    first, rows, _ = stream
-    index = [fixed.get(a, slice(None)) for a in "xzcy"]
-    return buf.at[(*index, pl.ds(first, rows), slice(None))]
+GATHER = ((0, 384), (1536, 384), (3072, 256))
+
+
+def region(buf, n, fixed, core=None):
+    first, width = GATHER[n]
+    start, size = (first + fixed["y"] * width, width) if "y" in fixed else (first, 4 * width)
+    index = [fixed.get(a, slice(None)) for a in "xz"] + ([] if core is None else [core])
+    return buf.at[(*index, slice(None), pl.ds(start, size))]
 
 
 def kernel(
-    list_ref, hidden_hbm, grad_out_hbm, live_ref, master_ref, moment_ref, variance_ref,
-    new_master_ref, new_moment_ref, new_variance_ref, clipped_ref, published,
-    hidden, grad_out, grad_out_t, acc, pair_part, sib_send, sib_recv,
+    list_hbm, hidden_hbm, grad_out_hbm, live_hbm, master_hbm, moment_hbm, variance_hbm,
+    new_master_hbm, new_moment_hbm, new_variance_hbm, clipped_hbm, published,
+    list_ref, hidden, grad_out, grad_out_t, live_ref, master_ref, moment_ref, variance_ref,
+    new_master_ref, new_moment_ref, new_variance_ref, clipped_ref, acc, pair_part, sib_send, sib_recv,
     send1a, recv1a, send1b, recv1b, send1c, recv1c,
     send2a, recv2a, send2b, recv2b, send2c, recv2c,
     send3a, recv3a, send3b, recv3b, send3c, recv3c,
-    turned, flat, sum_send, sum_recv,
-    load_sem, send_sem, recv_sem,
+    turned, flat, sum_send, sum_recv, swap_send, swap_recv, joined, held,
+    load_sem, store_sem, send_sem, recv_sem,
 ):
     me = where_am_i()
     px, py, pz, pc = me["x"], me["y"], me["z"], me["c"]
     loads = [
         pltpu.make_async_copy(grad_out_hbm, grad_out, load_sem.at[0]),
         pltpu.make_async_copy(hidden_hbm, hidden, load_sem.at[1]),
+        pltpu.make_async_copy(list_hbm, list_ref, load_sem.at[6]),
+        pltpu.make_async_copy(live_hbm, live_ref, load_sem.at[2]),
+        pltpu.make_async_copy(master_hbm, master_ref, load_sem.at[3]),
+        pltpu.make_async_copy(moment_hbm, moment_ref, load_sem.at[4]),
+        pltpu.make_async_copy(variance_hbm, variance_ref, load_sem.at[5]),
     ]
     for load in loads:
         load.start()
@@ -82,6 +92,7 @@
     for t in range(20):
         grad_out_t[pl.ds(t * 128, 128), :] = grad_out[:, t * 128 : (t + 1) * 128].T
     loads[1].wait()
+    loads[2].wait()
     pl.semaphore_wait(barrier, len(peers))
 
     issued = []
@@ -103,7 +114,7 @@
     def two_blocks(pair):
         both, odd = [], []
         for slot in (2 * pair, 2 * pair + 1):
-            row, column = list_ref[2 * slot], list_ref[2 * slot + 1]
+            row, column = list_ref[0, slot], list_ref[1, slot]
             left = grad_out_t[pl.ds(column * SIDE, SIDE), :]
             right = hidden[:, pl.ds((row >> 1) * 128, 128)]
             both.append(jnp.dot(left, right, preferred_element_type=F32))
@@ -232,7 +243,9 @@
     for add in last:
         add()
 
-    counts = live_ref[0:1, :]
+    for load in loads[3:]:
+        load.wait()
+    counts = live_ref[0:1, :].astype(F32)
     owner = ((px * 4 + pz) * 2 + pc) * 4 + py
     at = lax.broadcasted_iota(jnp.int32, (1, 128), 1)
     mine = jnp.sum(jnp.where(at == owner, counts, 0.0))
@@ -276,57 +289,94 @@
         new_moment_ref[:, at] = new_moment
         new_variance_ref[:, at] = new_variance
         new_master_ref[:, at] = new_master
-        turned[pl.ds(t, 4, 32), :] = new_master
-    published[px, pz, pc, py] = turned[...].astype(jnp.bfloat16)
-
-    def spread(stream, axis, fixed, d):
-        part = region(published, stream, 0, me, fixed)
-        return send(part, part, moved(me, **{axis: d}))
-
-    ready = []
-    for stream in (STREAMS[0], STREAMS[1], STREAMS[2]):
-        axis = stream[2][2]
-        ready.append([spread(stream, axis, {"x": px, "y": py, "z": pz, "c": pc}, d) for d in (2, 1, 3)])
-    for level in (1, 0):
-        for n, stream in enumerate(STREAMS):
-            for copy in ready[n]:
-                copy.wait_recv()
-            fixed = {"c": pc} | {a: me[a] for a in stream[2][: level + 1]}
-            axis = stream[2][level]
-            ready[n] = [spread(stream, axis, fixed, d) for d in (2, 1, 3)]
+        to, part = divmod(t, 3) if t < 12 else divmod(t - 12, 3) if t < 24 else divmod(t - 24, 2)
+        part += 0 if t < 12 else 3 if t < 24 else 6
+        swap_send[to, part // 2, pl.ds(4 * (part % 2), 4), :] = new_master
+    copies = [send(swap_send.at[(py + d) % 4], swap_recv.at[py], moved(me, y=d)) for d in (2, 1, 3)]
+    stores = []
+
+    def store(src, dst):
+        copy = pltpu.make_async_copy(src, dst, store_sem.at[len(stores)])
+        copy.start()
+        stores.append(copy)
+
+    store(new_master_ref, new_master_hbm)
+    store(new_moment_ref, new_moment_hbm)
+    store(new_variance_ref, new_variance_hbm)
+    store(clipped_ref, clipped_hbm)
+    swap_recv[py] = swap_send[py]
+    for copy in copies:
+        copy.wait_recv()
+    for part in range(8):
+        for source in range(4):
+            joined[part, pl.ds(4 * source, 4), :] = swap_recv[source, part // 2, pl.ds(4 * (part % 2), 4), :]
+    part = 0
+    for first, width in GATHER:
+        for column in range(0, width, 128):
+            at = pl.multiple_of(first + column + py * width, 128)
+            held[px, pz, :, pl.ds(at, 128)] = joined[part].astype(jnp.bfloat16)
+            part += 1
+
+    def spread(n, fixed, axis):
+        part = region(held, n, fixed)
+        return {d: send(part, part, moved(me, **{axis: d})) for d in (2, 1, 3)}
+
+    orders = [order for _, _, order in STREAMS]
+    inner = [spread(n, {"x": px, "y": py, "z": pz}, order[2]) for n, order in enumerate(orders)]
+    middle, outer = [], []
+    for n, order in enumerate(orders):
+        for copy in inner[n].values():
+            copy.wait_recv()
+        middle.append(spread(n, {a: me[a] for a in order[:2]}, order[1]))
+    for n, order in enumerate(orders):
+        outer.append([spread(n, {a: me[a] for a in order[:2]}, order[0])])
+    for d in (1, 3, 2):
+        for n, order in enumerate(orders):
+            middle[n][d].wait_recv()
+            outer[n].append(spread(n, {order[0]: me[order[0]], order[1]: (me[order[1]] - d) % 4}, order[0]))
     other = moved(me, c=1)
     passed = []
-    for stream in STREAMS:
-        part = region(published, stream, 0, me, {"c": pc, stream[2][0]: me[stream[2][0]]})
-        passed.append(send(part, part, other))
-    for m, d in enumerate((1, 3, 2)):
-        for n, stream in enumerate(STREAMS):
-            ready[n][(2, 1, 3).index(d)].wait_recv()
-            part = region(published, stream, 0, me, {"c": pc, stream[2][0]: (me[stream[2][0]] - d) % 4})
-            passed.append(send(part, part, other))
+
+    def settle(n, fixed):
+        part, place = region(held, n, fixed), region(published, n, fixed, pc)
+        passed.append(send(part, place, other))
+        store(part, place)
+
+    for n, order in enumerate(orders):
+        settle(n, {order[0]: me[order[0]]})
+    for d in (1, 3, 2):
+        for n, order in enumerate(orders):
+            for piece in outer[n]:
+                piece[d].wait_recv()
+            settle(n, {order[0]: (me[order[0]] - d) % 4})
     for copy in passed:
         copy.wait_recv()
     for copy in issued:
         copy.wait_send()
+    for copy in stores:
+        copy.wait()
 
 
 def local(hidden, grad_out, block_list, live_block_count, master, moment, variance):
     i16 = jnp.int16
     state = jax.ShapeDtypeStruct(master.shape, F32)
-    vmem, hbm = pl.BlockSpec(memory_space=pltpu.VMEM), pl.BlockSpec(memory_space=pl.ANY)
+    vmem, hbm = pl.BlockSpec(memory_space=pltpu.VMEM), pl.BlockSpec(memory_space=pltpu.HBM)
     first = [pltpu.VMEM((4, 3, 208, 128), i16)] * 4 + [pltpu.VMEM((3, 528, 128), i16)] * 2
     second = [pltpu.VMEM((3, 208, 128), i16)] * 4 + [pltpu.VMEM((3, 144, 128), i16)] * 2
     third = [pltpu.VMEM((3, 64, 128), i16)] * 4 + [pltpu.VMEM((3, 48, 128), i16)] * 2
-    copies = 4 + 27 + 18 + 22 + 27 + 12
+    copies = 4 + 27 + 18 + 22 + 3 + 9 + 9 + 36 + 12
     *updated, published = pl.pallas_call(
         kernel,
-        out_shape=[state] * 4 + [jax.ShapeDtypeStruct((4, 4, 2, 4, 128, 128), jnp.bfloat16)],
-        in_specs=[pl.BlockSpec(memory_space=pltpu.SMEM), hbm, hbm, vmem, vmem, vmem, vmem],
-        out_specs=[vmem] * 5,
+        out_shape=[state] * 4 + [jax.ShapeDtypeStruct((4, 4, 2, 16, 4096), jnp.bfloat16)],
+        in_specs=[hbm] * 7,
+        out_specs=[hbm] * 5,
         scratch_shapes=[
+            pltpu.SMEM(block_list.shape[::-1], jnp.int32),
             pltpu.VMEM(hidden.shape, jnp.bfloat16),
             pltpu.VMEM(grad_out.shape, jnp.bfloat16),
             pltpu.VMEM(grad_out.shape[::-1], jnp.bfloat16),
+            pltpu.VMEM((1, live_block_count.shape[0]), jnp.int32),
+            *[pltpu.VMEM(master.shape, F32)] * 7,
             pltpu.VMEM((4, 4, 4, 128, 128), F32),
             pltpu.VMEM((4, 4, 128, 128), F32),
             pltpu.VMEM((4, 2064, 128), i16),
@@ -336,18 +386,22 @@
             pltpu.VMEM((128, 128), F32),
             pltpu.VMEM((2, 8, 128), F32),
             pltpu.VMEM((22, 8, 128), F32),
-            pltpu.SemaphoreType.DMA((2,)),
+            pltpu.VMEM((4, 4, 8, 128), F32),
+            pltpu.VMEM((4, 4, 8, 128), F32),
+            pltpu.VMEM((8, 16, 128), F32),
+            pltpu.VMEM((4, 4, 16, 4096), jnp.bfloat16),
+            pltpu.SemaphoreType.DMA((7,)),
+            pltpu.SemaphoreType.DMA((16,)),
             pltpu.SemaphoreType.DMA((copies,)),
             pltpu.SemaphoreType.DMA((copies,)),
         ],
         compiler_params=pltpu.CompilerParams(
-            collective_id=0, has_side_effects=True, vmem_limit_bytes=48 * 2**20
+            collective_id=0, has_side_effects=True, vmem_limit_bytes=30 * 2**20
         ),
     )(
-        block_list.reshape(-1), hidden, grad_out,
-        live_block_count.astype(F32).reshape(1, -1), master, moment, variance,
+        *[pltpu.with_memory_space_constraint(a, pltpu.HBM) for a in (block_list.T, hidden, grad_out, live_block_count.reshape(1, -1), master, moment, variance)],
     )
-    return (*updated, published.reshape(master.shape[0] * 128, master.shape[1]))
+    return (*updated, published.reshape(512, 4096))
 
 
 def solution(mesh):

time: 87.4 us -> 74.5 us (0.85)
  local copies, waits for them, and re-layouts: 16.6 us -> 4.53 us
    reshape x2 -> x0, local copies, waits for them, and re-layouts: 7.44 us -> none  [the longest x1 7.28 us: local(): return (*updated, published.reshape(master.shape[0] * 128, master.shape[1]))]
    unnamed x15 -> x5, local copies, waits for them, and re-layouts: 9.17 us -> 4.53 us
where the time goes in v2:
time: 74.5 us; the launch traced here: 74.4 us
  Pallas kernels  69.2 us (93%)
  local copies, waits for them, and re-layouts  4.53 us (6%)
    pallas_call x1, Pallas kernels, local(): pl.pallas_call(kernel, out_shape=[state] * 4 + [jax.ShapeDtypeStruct((4,...  69.2 us
    unnamed x5, local copies, waits for them, and re-layouts  4.53 us

profile of v2, /device:TPU:1, one launch (start us, length us, event | category | flops | bytes accessed | tf_op | source)
XLA Modules:
  0.0 74.4 jit_solution(16275910635954175245)
XLA Ops:
  0.6 69.2 %shard_map.110 = (f32[4,4096]{1,0:T(4,128)S(1)}, f32[4,4096]{1,0:T(4,128)S(1)}, f32[4,4096]{1,0:T(4,128)S(1)}, f32[4,4096]{1,0:T(4,128)S(1)}, bf16[4,4,2,16,4096]{4,3,2,1,0:T(8,128)(2,1)S(1)}) custom-call(s32[2,512]{1,0:T(2,128)} %bitcast.4, bf16[256,6912]{1,0:T(8,128)(2,1)} %hidden_hbm.1, bf16[256,2560]{1,0:T(8,128)(2,1)} %grad_out_hbm.1, ...), custom_call_target="tpu_custom_call" | custom-call | tf_op jit(solution)/shard_map/pallas_call | solution.py:368
  69.9 0.6 copy.17
  70.5 0.6 copy.18
  71.1 0.6 copy.19
  71.7 0.6 copy.20
  72.4 2.0 %copy.21 = bf16[512,4096]{1,0:T(8,128)(2,1)} copy(bf16[512,4096]{1,0:T(8,128)(2,1)S(1)} %bitcast.3) | data formatting | bytes 8388608

commit v3 on v2

--- a/solution.py
+++ b/solution.py
@@ -53,6 +53,20 @@
     start, size = (first + fixed["y"] * width, width) if "y" in fixed else (first, 4 * width)
     index = [fixed.get(a, slice(None)) for a in "xz"] + ([] if core is None else [core])
     return buf.at[(*index, slice(None), pl.ds(start, size))]
+
+
+def part_of(t):
+    to, part = divmod(t, 3) if t < 12 else divmod(t - 12, 3) if t < 24 else divmod(t - 24, 2)
+    return to, part + (0 if t < 12 else 3 if t < 24 else 6)
+
+
+def adamw(clipped, master, moment, variance):
+    new_moment = 0.9 * moment + 0.1 * clipped
+    new_variance = 0.95 * variance + 0.05 * clipped * clipped
+    moment_hat = new_moment / (1.0 - 0.9**20)
+    variance_hat = new_variance / (1.0 - 0.95**20)
+    new_master = master - 0.02 * (moment_hat / (jnp.sqrt(variance_hat) + 1e-08) + 0.1 * master)
+    return new_master, new_moment, new_variance
 
 
 def kernel(
@@ -63,7 +77,7 @@
     send1a, recv1a, send1b, recv1b, send1c, recv1c,
     send2a, recv2a, send2b, recv2b, send2c, recv2c,
     send3a, recv3a, send3b, recv3b, send3c, recv3c,
-    turned, flat, sum_send, sum_recv, swap_send, swap_recv, joined, held,
+    turned, flat, sum_send, sum_recv, swap_send, swap_recv, state_send, state_recv, joined, held,
     load_sem, store_sem, send_sem, recv_sem,
 ):
     me = where_am_i()
@@ -91,6 +105,13 @@
     loads[0].wait()
     for t in range(20):
         grad_out_t[pl.ds(t * 128, 128), :] = grad_out[:, t * 128 : (t + 1) * 128].T
+    for load in loads[3:]:
+        load.wait()
+    for n, ref in enumerate((master_ref, moment_ref, variance_ref)):
+        for t in range(32):
+            to, part = part_of(t)
+            state_send[to, n, part // 2, pl.ds(4 * (part % 2), 4), :] = ref[:, t * 128 : (t + 1) * 128]
+    state_recv[py] = state_send[py]
     loads[1].wait()
     loads[2].wait()
     pl.semaphore_wait(barrier, len(peers))
@@ -107,6 +128,7 @@
         issued.append(copy)
         return copy
 
+    state_copies = [send(state_send.at[(py + d) % 4], state_recv.at[py], moved(me, y=d)) for d in (2, 1, 3)]
     lane = lax.broadcasted_iota(jnp.int32, (SIDE, 128), 1)
 
     low = lane < SIDE
@@ -243,8 +265,6 @@
     for add in last:
         add()
 
-    for load in loads[3:]:
-        load.wait()
     counts = live_ref[0:1, :].astype(F32)
     owner = ((px * 4 + pz) * 2 + pc) * 4 + py
     at = lax.broadcasted_iota(jnp.int32, (1, 128), 1)
@@ -260,6 +280,11 @@
     even, odd = turned[pl.ds(0, SIDE, 2), :], turned[pl.ds(1, SIDE, 2), :]
     flat[pl.ds(0, SIDE), :] = jnp.where(lane < SIDE, even, pltpu.roll(odd, SIDE, 1))
     flat[pl.ds(SIDE, SIDE), :] = jnp.where(lane < SIDE, pltpu.roll(even, SIDE, 1), odd)
+    for t in range(32):
+        to, part = part_of(t)
+        swap_send[to, part // 2, pl.ds(4 * (part % 2), 4), :] = flat[pl.ds(t, 4, 32), :]
+    swaps = [send(swap_send.at[(py + d) % 4], swap_recv.at[py], moved(me, y=d)) for d in (2, 1, 3)]
+    swap_recv[py] = swap_send[py]
     square = sum_send[0]
     for n, copy in enumerate(copies):
         copy.wait_recv()
@@ -273,26 +298,39 @@
     for n, copy in enumerate(copies):
         copy.wait_recv()
         square += sum_recv[7 + n]
-    mean_square = square[0:4] / live_total
+    for copy in swaps + state_copies:
+        copy.wait_recv()
+    mean_square = square / live_total
     clip = jnp.minimum(1.0, 1.0 / jnp.sqrt(mean_square + 1e-06))
 
+    for part in range(8):
+        for source in range(4):
+            rows, at = pl.ds(4 * source, 4), pl.ds(4 * (part % 2), 4)
+            joined[3, part, rows, :] = swap_recv[source, part // 2, at, :]
+            for n in range(3):
+                joined[n, part, rows, :] = state_recv[source, n, part // 2, at, :]
+    part = 0
+    for first, width in GATHER:
+        for column in range(0, width, 128):
+            at = pl.multiple_of(first + column + py * width, 128)
+            new_master, _, _ = adamw(clip[0:1] * joined[3, part], joined[0, part], joined[1, part], joined[2, part])
+            held[px, pz, :, pl.ds(at, 128)] = new_master.astype(jnp.bfloat16)
+            part += 1
+
+    def spread(n, fixed, axis):
+        part = region(held, n, fixed)
+        return {d: send(part, part, moved(me, **{axis: d})) for d in (2, 1, 3)}
+
+    orders = [order for _, _, order in STREAMS]
+    inner = [spread(n, {"x": px, "y": py, "z": pz}, order[2]) for n, order in enumerate(orders)]
     for t in range(32):
         at = pl.ds(t * 128, 128)
-        clipped = clip * flat[pl.ds(t, 4, 32), :]
-        new_moment = 0.9 * moment_ref[:, at] + 0.1 * clipped
-        new_variance = 0.95 * variance_ref[:, at] + 0.05 * clipped * clipped
-        moment_hat = new_moment / (1.0 - 0.9**20)
-        variance_hat = new_variance / (1.0 - 0.95**20)
-        master = master_ref[:, at]
-        new_master = master - 0.02 * (moment_hat / (jnp.sqrt(variance_hat) + 1e-08) + 0.1 * master)
+        clipped = clip[0:4] * flat[pl.ds(t, 4, 32), :]
+        new_master, new_moment, new_variance = adamw(clipped, master_ref[:, at], moment_ref[:, at], variance_ref[:, at])
         clipped_ref[:, at] = clipped
         new_moment_ref[:, at] = new_moment
         new_variance_ref[:, at] = new_variance
         new_master_ref[:, at] = new_master
-        to, part = divmod(t, 3) if t < 12 else divmod(t - 12, 3) if t < 24 else divmod(t - 24, 2)
-        part += 0 if t < 12 else 3 if t < 24 else 6
-        swap_send[to, part // 2, pl.ds(4 * (part % 2), 4), :] = new_master
-    copies = [send(swap_send.at[(py + d) % 4], swap_recv.at[py], moved(me, y=d)) for d in (2, 1, 3)]
     stores = []
 
     def store(src, dst):
@@ -304,25 +342,6 @@
     store(new_moment_ref, new_moment_hbm)
     store(new_variance_ref, new_variance_hbm)
     store(clipped_ref, clipped_hbm)
-    swap_recv[py] = swap_send[py]
-    for copy in copies:
-        copy.wait_recv()
-    for part in range(8):
-        for source in range(4):
-            joined[part, pl.ds(4 * source, 4), :] = swap_recv[source, part // 2, pl.ds(4 * (part % 2), 4), :]
-    part = 0
-    for first, width in GATHER:
-        for column in range(0, width, 128):
-            at = pl.multiple_of(first + column + py * width, 128)
-            held[px, pz, :, pl.ds(at, 128)] = joined[part].astype(jnp.bfloat16)
-            part += 1
-
-    def spread(n, fixed, axis):
-        part = region(held, n, fixed)
-        return {d: send(part, part, moved(me, **{axis: d})) for d in (2, 1, 3)}
-
-    orders = [order for _, _, order in STREAMS]
-    inner = [spread(n, {"x": px, "y": py, "z": pz}, order[2]) for n, order in enumerate(orders)]
     middle, outer = [], []
     for n, order in enumerate(orders):
         for copy in inner[n].values():
@@ -357,6 +376,19 @@
         copy.wait()
 
 
+def pass_on(*refs):
+    sources, results, sem = refs[:5], refs[5:10], refs[10]
+    copies = []
+    for i in range(4):
+        rows = pl.ds(i * 128, 128)
+        copies.append(pltpu.make_async_copy(sources[4].at[rows], results[4].at[rows], sem.at[i]))
+        copies.append(pltpu.make_async_copy(sources[i], results[i], sem.at[4 + i]))
+    for copy in copies:
+        copy.start()
+    for copy in copies:
+        copy.wait()
+
+
 def local(hidden, grad_out, block_list, live_block_count, master, moment, variance):
     i16 = jnp.int16
     state = jax.ShapeDtypeStruct(master.shape, F32)
@@ -364,7 +396,7 @@
     first = [pltpu.VMEM((4, 3, 208, 128), i16)] * 4 + [pltpu.VMEM((3, 528, 128), i16)] * 2
     second = [pltpu.VMEM((3, 208, 128), i16)] * 4 + [pltpu.VMEM((3, 144, 128), i16)] * 2
     third = [pltpu.VMEM((3, 64, 128), i16)] * 4 + [pltpu.VMEM((3, 48, 128), i16)] * 2
-    copies = 4 + 27 + 18 + 22 + 3 + 9 + 9 + 36 + 12
+    copies = 4 + 27 + 18 + 22 + 3 + 3 + 9 + 9 + 36 + 12
     *updated, published = pl.pallas_call(
         kernel,
         out_shape=[state] * 4 + [jax.ShapeDtypeStruct((4, 4, 2, 16, 4096), jnp.bfloat16)],
@@ -388,7 +420,9 @@
             pltpu.VMEM((22, 8, 128), F32),
             pltpu.VMEM((4, 4, 8, 128), F32),
             pltpu.VMEM((4, 4, 8, 128), F32),
-            pltpu.VMEM((8, 16, 128), F32),
+            pltpu.VMEM((4, 3, 4, 8, 128), F32),
+            pltpu.VMEM((4, 3, 4, 8, 128), F32),
+            pltpu.VMEM((4, 8, 16, 128), F32),
             pltpu.VMEM((4, 4, 16, 4096), jnp.bfloat16),
             pltpu.SemaphoreType.DMA((7,)),
             pltpu.SemaphoreType.DMA((16,)),
@@ -401,7 +435,14 @@
     )(
         *[pltpu.with_memory_space_constraint(a, pltpu.HBM) for a in (block_list.T, hidden, grad_out, live_block_count.reshape(1, -1), master, moment, variance)],
     )
-    return (*updated, published.reshape(512, 4096))
+    return pl.pallas_call(
+        pass_on,
+        out_shape=[state] * 4 + [jax.ShapeDtypeStruct((512, 4096), jnp.bfloat16)],
+        in_specs=[hbm] * 5,
+        out_specs=[hbm] * 5,
+        scratch_shapes=[pltpu.SemaphoreType.DMA((8,))],
+        compiler_params=pltpu.CompilerParams(vmem_limit_bytes=2**20),
+    )(*updated, published.reshape(512, 4096))
 
 
 def solution(mesh):

time: 74.5 us -> 68.6 us (0.921)
  local copies, waits for them, and re-layouts: 4.53 us -> 0 us
  Pallas kernels: 69.2 us -> 67.8 us
    unnamed x5 -> x0, local copies, waits for them, and re-layouts: 4.53 us -> none
    pallas_call x1, Pallas kernels: 69.2 us -> 65.7 us  [local(): pl.pallas_call(kernel, out_shape=[state] * 4 + [jax.ShapeDtypeStruct((4,...]
    pallas_call x0 -> x1, Pallas kernels: none -> 2.15 us  [local(): pl.pallas_call(pass_on, out_shape=[state] * 4 + [jax.ShapeDtypeStruct((51...]
where the time goes in v3:
time: 68.6 us; the launch traced here: 68.5 us
  Pallas kernels  67.8 us (99%)
    pallas_call x1, Pallas kernels, local(): pl.pallas_call(kernel, out_shape=[state] * 4 + [jax.ShapeDtypeStruct((4,...  65.7 us
    pallas_call x1, Pallas kernels, local(): pl.pallas_call(pass_on, out_shape=[state] * 4 + [jax.ShapeDtypeStruct((51...  2.15 us

profile of v3, /device:TPU:1, one launch (start us, length us, event | category | flops | bytes accessed | tf_op | source)
XLA Modules:
  0.0 68.5 jit_solution(2618541652947884324)
XLA Ops:
  0.6 65.7 %shard_map.110 = (f32[4,4096]{1,0:T(4,128)S(1)}, f32[4,4096]{1,0:T(4,128)S(1)}, f32[4,4096]{1,0:T(4,128)S(1)}, f32[4,4096]{1,0:T(4,128)S(1)}, bf16[4,4,2,16,4096]{4,3,2,1,0:T(8,128)(2,1)S(1)}) custom-call(s32[2,512]{1,0:T(2,128)} %bitcast.4, bf16[256,6912]{1,0:T(8,128)(2,1)} %hidden_hbm.1, bf16[256,2560]{1,0:T(8,128)(2,1)} %grad_out_hbm.1, ...), custom_call_target="tpu_custom_call" | custom-call | tf_op jit(solution)/shard_map/pallas_call | solution.py:400
  66.3 2.1 %shard_map.111 = (f32[4,4096]{1,0:T(4,128)}, f32[4,4096]{1,0:T(4,128)}, f32[4,4096]{1,0:T(4,128)}, f32[4,4096]{1,0:T(4,128)}, bf16[512,4096]{1,0:T(8,128)(2,1)}) custom-call(f32[4,4096]{1,0:T(4,128)S(1)} %get-tuple-element.10.refs_0_, f32[4,4096]{1,0:T(4,128)S(1)} %get-tuple-element.11.refs_1_, f32[4,4096]{1,0:T(4,128)S(1)} %get-tuple-element.12.refs_2_, ...), custom_call_target="tpu_custom_call" | custom-call | tf_op jit(solution)/shard_map/pallas_call | solution.py:438

commit v4 on v3

--- a/solution.py
+++ b/solution.py
@@ -9,7 +9,7 @@
 
 MESH = pl.DeviceIdType.MESH
 SIDE = 64
-TOKENS = 256
+UNROLL = 32
 SLAB_ORDER = (2, 1, 3, 0)
 STREAMS = ((0, 48, "xyz"), (48, 48, "yzx"), (96, 32, "zxy"))
 F32 = jnp.float32
@@ -82,6 +82,14 @@
 ):
     me = where_am_i()
     px, py, pz, pc = me["x"], me["y"], me["z"], me["c"]
+    peers = [moved(me, c=1)]
+    peers += [moved(me, **{a: d}) for a in "xyz" for d in (1, 2, 3)]
+    peers += [moved(me, x=d, c=1) for d in (1, 2, 3)]
+    peers += [moved(me, y=i, z=j) for i in (1, 2, 3) for j in (1, 2, 3)]
+    barrier = pltpu.get_barrier_semaphore()
+    for peer in peers:
+        pl.semaphore_signal(barrier, inc=1, device_id=device_at(peer), device_id_type=MESH)
+
     loads = [
         pltpu.make_async_copy(grad_out_hbm, grad_out, load_sem.at[0]),
         pltpu.make_async_copy(hidden_hbm, hidden, load_sem.at[1]),
@@ -94,24 +102,9 @@
     for load in loads:
         load.start()
 
-    peers = [moved(me, c=1)]
-    peers += [moved(me, **{a: d}) for a in "xyz" for d in (1, 2, 3)]
-    peers += [moved(me, x=d, c=1) for d in (1, 2, 3)]
-    peers += [moved(me, y=i, z=j) for i in (1, 2, 3) for j in (1, 2, 3)]
-    barrier = pltpu.get_barrier_semaphore()
-    for peer in peers:
-        pl.semaphore_signal(barrier, inc=1, device_id=device_at(peer), device_id_type=MESH)
-
     loads[0].wait()
     for t in range(20):
         grad_out_t[pl.ds(t * 128, 128), :] = grad_out[:, t * 128 : (t + 1) * 128].T
-    for load in loads[3:]:
-        load.wait()
-    for n, ref in enumerate((master_ref, moment_ref, variance_ref)):
-        for t in range(32):
-            to, part = part_of(t)
-            state_send[to, n, part // 2, pl.ds(4 * (part % 2), 4), :] = ref[:, t * 128 : (t + 1) * 128]
-    state_recv[py] = state_send[py]
     loads[1].wait()
     loads[2].wait()
     pl.semaphore_wait(barrier, len(peers))
@@ -128,7 +121,6 @@
         issued.append(copy)
         return copy
 
-    state_copies = [send(state_send.at[(py + d) % 4], state_recv.at[py], moved(me, y=d)) for d in (2, 1, 3)]
     lane = lax.broadcasted_iota(jnp.int32, (SIDE, 128), 1)
 
     low = lane < SIDE
@@ -145,37 +137,57 @@
         straight = jnp.where(low, both[0], both[1])
         return jnp.where(jnp.where(low, odd[0], 1 - odd[1]) == 1, crossed, straight)
 
-    sends1 = []
-    for k, step in enumerate(SLAB_ORDER):
-        zk = (pz + step) % 4
-
-        def for_sibling(i, top, zk=zk):
-            for u in range(16):
-                x, y, p = 2 * i + u // 8, (u // 2) % 4, u % 2
+    def swap_state():
+        for load in loads[3:]:
+            load.wait()
+        for n, ref in enumerate((master_ref, moment_ref, variance_ref)):
+            for t in range(32):
+                to, part = part_of(t)
+                state_send[to, n, part // 2, pl.ds(4 * (part % 2), 4), :] = ref[:, t * 128 : (t + 1) * 128]
+        state_recv[py] = state_send[py]
+        return [send(state_send.at[(py + d) % 4], state_recv.at[py], moved(me, y=d)) for d in (2, 1, 3)]
+
+    sends1, to_sibling = [], []
+
+    def first_half(k):
+        zk = (pz + SLAB_ORDER[k]) % 4
+
+        def for_sibling(i, top):
+            for u in range(UNROLL):
+                n = UNROLL * i + u
+                x, y, p = n // 8, (n // 2) % 4, n % 2
                 owner = ((x * 4 + zk) * 2 + (1 - pc)) * 4 + y
                 part = two_blocks(2 * owner + p)
                 pair_part[x, y, pl.ds(p * SIDE, SIDE), :] = part
                 top = jnp.maximum(top, jnp.max(jnp.abs(part).reshape(8, 8, 128), axis=0))
             return top
 
-        top = lax.fori_loop(0, 2, for_sibling, jnp.zeros((8, 128), F32))
+        top = lax.fori_loop(0, 32 // UNROLL, for_sibling, jnp.zeros((8, 128), F32))
         exponent = exponent_of(top)
         inverse = jnp.exp2(-exponent)[0:1, :]
         for x in range(4):
             for y in range(4):
                 sib_send[k, pl.ds((x * 4 + y) * 128, 128), :] = encode(pair_part[x, y], inverse)
         sib_send[k, pl.ds(2048, 16), :] = exponent.astype(jnp.int32).astype(jnp.int16)
-        sib = send(sib_send.at[k], sib_recv.at[k], moved(me, c=1))
-
-        def for_self(i, carry, zk=zk):
-            for u in range(16):
-                x, y, p = 2 * i + u // 8, (u // 2) % 4, u % 2
+        to_sibling.append(send(sib_send.at[k], sib_recv.at[k], moved(me, c=1)))
+
+    def second_half(k):
+        zk = (pz + SLAB_ORDER[k]) % 4
+
+        def for_self(i, carry):
+            for u in range(UNROLL):
+                n = UNROLL * i + u
+                x, y, p = n // 8, (n // 2) % 4, n % 2
                 owner = ((x * 4 + zk) * 2 + pc) * 4 + y
                 acc[x, zk, y, pl.ds(p * SIDE, SIDE), :] = two_blocks(2 * owner + p)
             return carry
 
-        lax.fori_loop(0, 2, for_self, 0)
-        sib.wait_recv()
+        lax.fori_loop(0, 32 // UNROLL, for_self, 0)
+
+    def join(k):
+        step = SLAB_ORDER[k]
+        zk = (pz + step) % 4
+        to_sibling[k].wait_recv()
         scale = jnp.exp2(splat(sib_recv[k, pl.ds(2048, 16), :]))
         top = jnp.zeros((8, 128), F32)
         for x in range(4):
@@ -205,6 +217,14 @@
             send1b[k, d - 1, pl.ds(192, 16), :] = exponent
             slab.append(send(send1b.at[k, d - 1], recv1b.at[k, d - 1], moved(me, y=d)))
         sends1.append(slab)
+
+    first_half(0)
+    state_copies = swap_state()
+    for k in range(4):
+        second_half(k)
+        if k < 3:
+            first_half(k + 1)
+        join(k)
 
     def finish(k):
         step = SLAB_ORDER[k]
@@ -363,11 +383,15 @@
 
     for n, order in enumerate(orders):
         settle(n, {order[0]: me[order[0]]})
-    for d in (1, 3, 2):
+    for d in (1, 3):
         for n, order in enumerate(orders):
             for piece in outer[n]:
                 piece[d].wait_recv()
             settle(n, {order[0]: (me[order[0]] - d) % 4})
+    for m, e in enumerate((0, 1, 3, 2)):
+        for n, order in enumerate(orders):
+            outer[n][m][2].wait_recv()
+            settle(n, {order[0]: (me[order[0]] - 2) % 4, order[1]: (me[order[1]] - e) % 4})
     for copy in passed:
         copy.wait_recv()
     for copy in issued:
@@ -396,7 +420,7 @@
     first = [pltpu.VMEM((4, 3, 208, 128), i16)] * 4 + [pltpu.VMEM((3, 528, 128), i16)] * 2
     second = [pltpu.VMEM((3, 208, 128), i16)] * 4 + [pltpu.VMEM((3, 144, 128), i16)] * 2
     third = [pltpu.VMEM((3, 64, 128), i16)] * 4 + [pltpu.VMEM((3, 48, 128), i16)] * 2
-    copies = 4 + 27 + 18 + 22 + 3 + 3 + 9 + 9 + 36 + 12
+    copies = 4 + 27 + 18 + 22 + 3 + 3 + 9 + 9 + 36 + 21
     *updated, published = pl.pallas_call(
         kernel,
         out_shape=[state] * 4 + [jax.ShapeDtypeStruct((4, 4, 2, 16, 4096), jnp.bfloat16)],
@@ -425,7 +449,7 @@
             pltpu.VMEM((4, 8, 16, 128), F32),
             pltpu.VMEM((4, 4, 16, 4096), jnp.bfloat16),
             pltpu.SemaphoreType.DMA((7,)),
-            pltpu.SemaphoreType.DMA((16,)),
+            pltpu.SemaphoreType.DMA((25,)),
             pltpu.SemaphoreType.DMA((copies,)),
             pltpu.SemaphoreType.DMA((copies,)),
         ],

time: 68.6 us -> 66.6 us (0.971)
  Pallas kernels: 67.8 us -> 65.8 us
    pallas_call x1, Pallas kernels: 65.7 us -> 63.7 us  [local(): pl.pallas_call(kernel, out_shape=[state] * 4 + [jax.ShapeDtypeStruct((4,...]
where the time goes in v4:
time: 66.6 us; the launch traced here: 66.5 us
  Pallas kernels  65.8 us (99%)
    pallas_call x1, Pallas kernels, local(): pl.pallas_call(kernel, out_shape=[state] * 4 + [jax.ShapeDtypeStruct((4,...  63.7 us
    pallas_call x1, Pallas kernels, local(): pl.pallas_call(pass_on, out_shape=[state] * 4 + [jax.ShapeDtypeStruct((51...  2.15 us

profile of v4, /device:TPU:1, one launch (start us, length us, event | category | flops | bytes accessed | tf_op | source)
XLA Modules:
  0.0 66.5 jit_solution(4082599260203767568)
XLA Ops:
  0.6 63.7 %shard_map.110 = (f32[4,4096]{1,0:T(4,128)S(1)}, f32[4,4096]{1,0:T(4,128)S(1)}, f32[4,4096]{1,0:T(4,128)S(1)}, f32[4,4096]{1,0:T(4,128)S(1)}, bf16[4,4,2,16,4096]{4,3,2,1,0:T(8,128)(2,1)S(1)}) custom-call(s32[2,512]{1,0:T(2,128)} %bitcast.4, bf16[256,6912]{1,0:T(8,128)(2,1)} %hidden_hbm.1, bf16[256,2560]{1,0:T(8,128)(2,1)} %grad_out_hbm.1, ...), custom_call_target="tpu_custom_call" | custom-call | tf_op jit(solution)/shard_map/pallas_call | solution.py:424
  64.3 2.1 %shard_map.111 = (f32[4,4096]{1,0:T(4,128)}, f32[4,4096]{1,0:T(4,128)}, f32[4,4096]{1,0:T(4,128)}, f32[4,4096]{1,0:T(4,128)}, bf16[512,4096]{1,0:T(8,128)(2,1)}) custom-call(f32[4,4096]{1,0:T(4,128)S(1)} %get-tuple-element.10.refs_0_, f32[4,4096]{1,0:T(4,128)S(1)} %get-tuple-element.11.refs_1_, f32[4,4096]{1,0:T(4,128)S(1)} %get-tuple-element.12.refs_2_, ...), custom_call_target="tpu_custom_call" | custom-call | tf_op jit(solution)/shard_map/pallas_call | solution.py:462

commit v5 on v4

--- a/solution.py
+++ b/solution.py
@@ -282,17 +282,18 @@
     last.append(later_phase("z", send3a, recv3a, 48, 0, 1, lambda j, q: (px, q, py)))
     adds[2]()
     last.append(later_phase("x", send3b, recv3b, 48, 48, 1, lambda j, q: (q, pz, py)))
-    for add in last:
-        add()
-
     counts = live_ref[0:1, :].astype(F32)
     owner = ((px * 4 + pz) * 2 + pc) * 4 + py
     at = lax.broadcasted_iota(jnp.int32, (1, 128), 1)
     mine = jnp.sum(jnp.where(at == owner, counts, 0.0))
     live_total = jnp.sum(counts) * float(SIDE * SIDE)
     slot = 2 * (lax.broadcasted_iota(jnp.int32, (128, 128), 0) // SIDE) + lax.broadcasted_iota(jnp.int32, (128, 128), 1) // SIDE
-    own = jnp.where(slot.astype(F32) < mine, acc[px, pz, py], 0.0)
-    sum_send[0] = jnp.full((8, 128), jnp.sum(own * own), F32)
+    live = slot.astype(F32) < mine
+    for add in last:
+        add()
+
+    own = jnp.where(live, acc[px, pz, py], 0.0)
+    sum_send[0] = jnp.full((1, 128), jnp.sum(own * own), F32)
     copies = []
     for n, by in enumerate([{"c": 1}] + [{"x": d, "c": c} for d in (1, 2, 3) for c in (0, 1)]):
         copies.append(send(sum_send.at[0], sum_recv.at[n], moved(me, **by)))
@@ -337,15 +338,15 @@
             held[px, pz, :, pl.ds(at, 128)] = new_master.astype(jnp.bfloat16)
             part += 1
 
-    def spread(n, fixed, axis):
+    def spread(n, fixed, axis, steps=(2, 1, 3)):
         part = region(held, n, fixed)
-        return {d: send(part, part, moved(me, **{axis: d})) for d in (2, 1, 3)}
+        return {d: send(part, part, moved(me, **{axis: d})) for d in steps}
 
     orders = [order for _, _, order in STREAMS]
     inner = [spread(n, {"x": px, "y": py, "z": pz}, order[2]) for n, order in enumerate(orders)]
     for t in range(32):
         at = pl.ds(t * 128, 128)
-        clipped = clip[0:4] * flat[pl.ds(t, 4, 32), :]
+        clipped = clip * flat[pl.ds(t, 4, 32), :]
         new_master, new_moment, new_variance = adamw(clipped, master_ref[:, at], moment_ref[:, at], variance_ref[:, at])
         clipped_ref[:, at] = clipped
         new_moment_ref[:, at] = new_moment
@@ -362,17 +363,35 @@
     store(new_moment_ref, new_moment_hbm)
     store(new_variance_ref, new_variance_hbm)
     store(clipped_ref, clipped_hbm)
-    middle, outer = [], []
+    middle = []
     for n, order in enumerate(orders):
         for copy in inner[n].values():
             copy.wait_recv()
         middle.append(spread(n, {a: me[a] for a in order[:2]}, order[1]))
-    for n, order in enumerate(orders):
-        outer.append([spread(n, {a: me[a] for a in order[:2]}, order[0])])
-    for d in (1, 3, 2):
+    turns = (0, 1, 3, 2)
+    outer, beyond = [[] for _ in orders], [{} for _ in orders]
+
+    def outward(m):
         for n, order in enumerate(orders):
-            middle[n][d].wait_recv()
-            outer[n].append(spread(n, {order[0]: me[order[0]], order[1]: (me[order[1]] - d) % 4}, order[0]))
+            if m:
+                middle[n][turns[m]].wait_recv()
+            fixed = {order[0]: me[order[0]], order[1]: (me[order[1]] - turns[m]) % 4}
+            outer[n].append(spread(n, fixed, order[0], (1, 3)))
+
+    def onward(m):
+        d = 1 if m < 2 else 3
+        for n, order in enumerate(orders):
+            outer[n][m].pop(d).wait_recv()
+            fixed = {order[0]: (me[order[0]] - d) % 4, order[1]: (me[order[1]] - turns[m]) % 4}
+            beyond[n].update({m: spread(n, fixed, order[0], (d,))[d]})
+
+    outward(0)
+    outward(1)
+    onward(0)
+    outward(2)
+    outward(3)
+    for m in (1, 2, 3):
+        onward(m)
     other = moved(me, c=1)
     passed = []
 
@@ -386,12 +405,13 @@
     for d in (1, 3):
         for n, order in enumerate(orders):
             for piece in outer[n]:
-                piece[d].wait_recv()
+                if d in piece:
+                    piece[d].wait_recv()
             settle(n, {order[0]: (me[order[0]] - d) % 4})
-    for m, e in enumerate((0, 1, 3, 2)):
+    for m in range(4):
         for n, order in enumerate(orders):
-            outer[n][m][2].wait_recv()
-            settle(n, {order[0]: (me[order[0]] - 2) % 4, order[1]: (me[order[1]] - e) % 4})
+            beyond[n][m].wait_recv()
+            settle(n, {order[0]: (me[order[0]] - 2) % 4, order[1]: (me[order[1]] - turns[m]) % 4})
     for copy in passed:
         copy.wait_recv()
     for copy in issued:
@@ -440,8 +460,8 @@
             *first, *second, *third,
             pltpu.VMEM((128, 128), F32),
             pltpu.VMEM((128, 128), F32),
-            pltpu.VMEM((2, 8, 128), F32),
-            pltpu.VMEM((22, 8, 128), F32),
+            pltpu.VMEM((2, 1, 128), F32),
+            pltpu.VMEM((22, 1, 128), F32),
             pltpu.VMEM((4, 4, 8, 128), F32),
             pltpu.VMEM((4, 4, 8, 128), F32),
             pltpu.VMEM((4, 3, 4, 8, 128), F32),

time: 66.6 us -> 64.8 us (0.973)
  Pallas kernels: 65.8 us -> 64.1 us
    pallas_call x1, Pallas kernels: 63.7 us -> 61.9 us  [local(): pl.pallas_call(kernel, out_shape=[state] * 4 + [jax.ShapeDtypeStruct((4,...]
where the time goes in v5:
time: 64.8 us; the launch traced here: 64.7 us
  Pallas kernels  64.1 us (99%)
    pallas_call x1, Pallas kernels, local(): pl.pallas_call(kernel, out_shape=[state] * 4 + [jax.ShapeDtypeStruct((4,...  61.9 us
    pallas_call x1, Pallas kernels, local(): pl.pallas_call(pass_on, out_shape=[state] * 4 + [jax.ShapeDtypeStruct((51...  2.15 us

profile of v5, /device:TPU:1, one launch (start us, length us, event | category | flops | bytes accessed | tf_op | source)
XLA Modules:
  0.0 64.7 jit_solution(14606262029875280729)
XLA Ops:
  0.6 61.9 %shard_map.110 = (f32[4,4096]{1,0:T(4,128)S(1)}, f32[4,4096]{1,0:T(4,128)S(1)}, f32[4,4096]{1,0:T(4,128)S(1)}, f32[4,4096]{1,0:T(4,128)S(1)}, bf16[4,4,2,16,4096]{4,3,2,1,0:T(8,128)(2,1)S(1)}) custom-call(s32[2,512]{1,0:T(2,128)} %bitcast.4, bf16[256,6912]{1,0:T(8,128)(2,1)} %hidden_hbm.1, bf16[256,2560]{1,0:T(8,128)(2,1)} %grad_out_hbm.1, ...), custom_call_target="tpu_custom_call" | custom-call | tf_op jit(solution)/shard_map/pallas_call | solution.py:444
  62.6 2.1 %shard_map.111 = (f32[4,4096]{1,0:T(4,128)}, f32[4,4096]{1,0:T(4,128)}, f32[4,4096]{1,0:T(4,128)}, f32[4,4096]{1,0:T(4,128)}, bf16[512,4096]{1,0:T(8,128)(2,1)}) custom-call(f32[4,4096]{1,0:T(4,128)S(1)} %get-tuple-element.10.refs_0_, f32[4,4096]{1,0:T(4,128)S(1)} %get-tuple-element.11.refs_1_, f32[4,4096]{1,0:T(4,128)S(1)} %get-tuple-element.12.refs_2_, ...), custom_call_target="tpu_custom_call" | custom-call | tf_op jit(solution)/shard_map/pallas_call | solution.py:482

commit v6 on v5

--- a/solution.py
+++ b/solution.py
@@ -91,7 +91,6 @@
         pl.semaphore_signal(barrier, inc=1, device_id=device_at(peer), device_id_type=MESH)
 
     loads = [
-        pltpu.make_async_copy(grad_out_hbm, grad_out, load_sem.at[0]),
         pltpu.make_async_copy(hidden_hbm, hidden, load_sem.at[1]),
         pltpu.make_async_copy(list_hbm, list_ref, load_sem.at[6]),
         pltpu.make_async_copy(live_hbm, live_ref, load_sem.at[2]),
@@ -99,14 +98,17 @@
         pltpu.make_async_copy(moment_hbm, moment_ref, load_sem.at[4]),
         pltpu.make_async_copy(variance_hbm, variance_ref, load_sem.at[5]),
     ]
-    for load in loads:
+    quarters = [pl.ds(q * (grad_out.shape[1] // 4), grad_out.shape[1] // 4) for q in range(4)]
+    pieces = [pltpu.make_async_copy(grad_out_hbm.at[:, q], grad_out.at[:, q], load_sem.at[7 + i]) for i, q in enumerate(quarters)]
+    for load in pieces + loads:
         load.start()
 
+    for t in range(20):
+        if t % 5 == 0:
+            pieces[t // 5].wait()
+        grad_out_t[pl.ds(t * 128, 128), :] = grad_out[:, t * 128 : (t + 1) * 128].T
     loads[0].wait()
-    for t in range(20):
-        grad_out_t[pl.ds(t * 128, 128), :] = grad_out[:, t * 128 : (t + 1) * 128].T
     loads[1].wait()
-    loads[2].wait()
     pl.semaphore_wait(barrier, len(peers))
 
     issued = []
@@ -138,7 +140,7 @@
         return jnp.where(jnp.where(low, odd[0], 1 - odd[1]) == 1, crossed, straight)
 
     def swap_state():
-        for load in loads[3:]:
+        for load in loads[2:]:
             load.wait()
         for n, ref in enumerate((master_ref, moment_ref, variance_ref)):
             for t in range(32):
@@ -246,9 +248,6 @@
             for x in range(4):
                 acc[x, zk, py, 48:96, :] += scale * recv1b[k, d - 1, pl.ds(x * 48, 48), :].astype(F32)
 
-    for k in range(4):
-        finish(k)
-
     def later_phase(axis, out_buf, in_buf, rows, first, count, place):
         held = [[acc[(*place(j, (me[axis] + d) % 4), pl.ds(first, rows), slice(None))] for j in range(count)] for d in (2, 1, 3)]
         top = functools.reduce(jnp.maximum, [jnp.max(jnp.abs(v).reshape(rows // 8, 8, 128), axis=0) for h in held for v in h])
@@ -271,8 +270,11 @@
 
         return add
 
-    adds = [
-        later_phase("x", send2c, recv2c, 32, 96, 4, lambda j, q: (q, pz, j)),
+    for k in range(3):
+        finish(k)
+    adds = [later_phase("x", send2c, recv2c, 32, 96, 4, lambda j, q: (q, pz, j))]
+    finish(3)
+    adds += [
         later_phase("y", send2a, recv2a, 48, 0, 4, lambda j, q: (px, j, q)),
         later_phase("z", send2b, recv2b, 48, 48, 4, lambda j, q: (j, q, py)),
     ]
@@ -295,7 +297,7 @@
     own = jnp.where(live, acc[px, pz, py], 0.0)
     sum_send[0] = jnp.full((1, 128), jnp.sum(own * own), F32)
     copies = []
-    for n, by in enumerate([{"c": 1}] + [{"x": d, "c": c} for d in (1, 2, 3) for c in (0, 1)]):
+    for n, by in enumerate([{"x": d, "c": c} for d in (2, 1, 3) for c in (1, 0)] + [{"c": 1}]):
         copies.append(send(sum_send.at[0], sum_recv.at[n], moved(me, **by)))
     turned[...] = own.T
     even, odd = turned[pl.ds(0, SIDE, 2), :], turned[pl.ds(1, SIDE, 2), :]
@@ -312,8 +314,8 @@
         square += sum_recv[n]
     sum_send[1] = square
     copies = []
-    for i in range(4):
-        for j in range(4):
+    for i in (2, 1, 3, 0):
+        for j in (2, 1, 3, 0):
             if i or j:
                 copies.append(send(sum_send.at[1], sum_recv.at[7 + len(copies)], moved(me, y=i, z=j)))
     for n, copy in enumerate(copies):
@@ -468,7 +470,7 @@
             pltpu.VMEM((4, 3, 4, 8, 128), F32),
             pltpu.VMEM((4, 8, 16, 128), F32),
             pltpu.VMEM((4, 4, 16, 4096), jnp.bfloat16),
-            pltpu.SemaphoreType.DMA((7,)),
+            pltpu.SemaphoreType.DMA((11,)),
             pltpu.SemaphoreType.DMA((25,)),
             pltpu.SemaphoreType.DMA((copies,)),
             pltpu.SemaphoreType.DMA((copies,)),

time: 64.8 us -> 65 us (level)
  no operation moved by 1% of the time
where the time goes in v6:
time: 65 us; the launch traced here: 64.9 us
  Pallas kernels  64.3 us (99%)
    pallas_call x1, Pallas kernels, local(): pl.pallas_call(kernel, out_shape=[state] * 4 + [jax.ShapeDtypeStruct((4,...  62.1 us
    pallas_call x1, Pallas kernels, local(): pl.pallas_call(pass_on, out_shape=[state] * 4 + [jax.ShapeDtypeStruct((51...  2.15 us

profile of v6, /device:TPU:1, one launch (start us, length us, event | category | flops | bytes accessed | tf_op | source)
XLA Modules:
  0.0 64.9 jit_solution(11439682667239588486)
XLA Ops:
  0.6 62.1 %shard_map.110 = (f32[4,4096]{1,0:T(4,128)S(1)}, f32[4,4096]{1,0:T(4,128)S(1)}, f32[4,4096]{1,0:T(4,128)S(1)}, f32[4,4096]{1,0:T(4,128)S(1)}, bf16[4,4,2,16,4096]{4,3,2,1,0:T(8,128)(2,1)S(1)}) custom-call(s32[2,512]{1,0:T(2,128)} %bitcast.4, bf16[256,6912]{1,0:T(8,128)(2,1)} %hidden_hbm.1, bf16[256,2560]{1,0:T(8,128)(2,1)} %grad_out_hbm.1, ...), custom_call_target="tpu_custom_call" | custom-call | tf_op jit(solution)/shard_map/pallas_call | solution.py:446
  62.8 2.1 %shard_map.111 = (f32[4,4096]{1,0:T(4,128)}, f32[4,4096]{1,0:T(4,128)}, f32[4,4096]{1,0:T(4,128)}, f32[4,4096]{1,0:T(4,128)}, bf16[512,4096]{1,0:T(8,128)(2,1)}) custom-call(f32[4,4096]{1,0:T(4,128)S(1)} %get-tuple-element.10.refs_0_, f32[4,4096]{1,0:T(4,128)S(1)} %get-tuple-element.11.refs_1_, f32[4,4096]{1,0:T(4,128)S(1)} %get-tuple-element.12.refs_2_, ...), custom_call_target="tpu_custom_call" | custom-call | tf_op jit(solution)/shard_map/pallas_call | solution.py:484

commit v7 on v5

--- a/solution.py
+++ b/solution.py
@@ -385,23 +385,24 @@
             fixed = {order[0]: (me[order[0]] - d) % 4, order[1]: (me[order[1]] - turns[m]) % 4}
             beyond[n].update({m: spread(n, fixed, order[0], (d,))[d]})
 
+    other = moved(me, c=1)
+    passed = []
+
+    def settle(n, fixed):
+        part, place = region(held, n, fixed), region(published, n, fixed, pc)
+        passed.append(send(part, place, other))
+        store(part, place)
+
     outward(0)
     outward(1)
     onward(0)
     outward(2)
     outward(3)
-    for m in (1, 2, 3):
-        onward(m)
-    other = moved(me, c=1)
-    passed = []
-
-    def settle(n, fixed):
-        part, place = region(held, n, fixed), region(published, n, fixed, pc)
-        passed.append(send(part, place, other))
-        store(part, place)
-
+    onward(1)
     for n, order in enumerate(orders):
         settle(n, {order[0]: me[order[0]]})
+    for m in (2, 3):
+        onward(m)
     for d in (1, 3):
         for n, order in enumerate(orders):
             for piece in outer[n]:

time: 64.8 us -> 64.9 us (level)
  no operation moved by 1% of the time
where the time goes in v7:
time: 64.9 us; the launch traced here: 64.8 us
  Pallas kernels  64.1 us (99%)
    pallas_call x1, Pallas kernels, local(): pl.pallas_call(kernel, out_shape=[state] * 4 + [jax.ShapeDtypeStruct((4,...  62 us
    pallas_call x1, Pallas kernels, local(): pl.pallas_call(pass_on, out_shape=[state] * 4 + [jax.ShapeDtypeStruct((51...  2.15 us

profile of v7, /device:TPU:1, one launch (start us, length us, event | category | flops | bytes accessed | tf_op | source)
XLA Modules:
  0.0 64.8 jit_solution(14361225323005551964)
XLA Ops:
  0.6 62.0 %shard_map.110 = (f32[4,4096]{1,0:T(4,128)S(1)}, f32[4,4096]{1,0:T(4,128)S(1)}, f32[4,4096]{1,0:T(4,128)S(1)}, f32[4,4096]{1,0:T(4,128)S(1)}, bf16[4,4,2,16,4096]{4,3,2,1,0:T(8,128)(2,1)S(1)}) custom-call(s32[2,512]{1,0:T(2,128)} %bitcast.4, bf16[256,6912]{1,0:T(8,128)(2,1)} %hidden_hbm.1, bf16[256,2560]{1,0:T(8,128)(2,1)} %grad_out_hbm.1, ...), custom_call_target="tpu_custom_call" | custom-call | tf_op jit(solution)/shard_map/pallas_call | solution.py:445
  62.6 2.1 %shard_map.111 = (f32[4,4096]{1,0:T(4,128)}, f32[4,4096]{1,0:T(4,128)}, f32[4,4096]{1,0:T(4,128)}, f32[4,4096]{1,0:T(4,128)}, bf16[512,4096]{1,0:T(8,128)(2,1)}) custom-call(f32[4,4096]{1,0:T(4,128)S(1)} %get-tuple-element.10.refs_0_, f32[4,4096]{1,0:T(4,128)S(1)} %get-tuple-element.11.refs_1_, f32[4,4096]{1,0:T(4,128)S(1)} %get-tuple-element.12.refs_2_, ...), custom_call_target="tpu_custom_call" | custom-call | tf_op jit(solution)/shard_map/pallas_call | solution.py:483
